TPU v7x, 32 devices: a whole 2x2x4 slice. The times are simulated.
32 devices in a mesh: dp: 16 (over z, y, x), tp: 2 (over core).
Axes of the slice: x: 2, y: 2, z: 4, core: 2. Of those that a mesh axis runs over, the one named last changes fastest.
Arguments:
- tokens: bfloat16 [32768, 768], P(('dp', 'tp')), may hold values from -6 to 6
- cotangent: bfloat16 [32768, 768], P(('dp', 'tp')), may hold values from -6 to 6
- lengths: int32 [16, 8], P('dp'), may hold values from 0 to 2048, as said below
- qkv_weight: bfloat16 [768, 2304], P(('dp', 'tp')), may hold values from -0.21875 to 0.21875
- out_weight: bfloat16 [768, 768], P(('dp', 'tp')), may hold values from -0.21875 to 0.21875
- pre_gain: bfloat16 [768], P(('dp', 'tp')), may hold values from 0.25 to 1.75
- pre_shift: bfloat16 [768], P(('dp', 'tp')), may hold values from -2 to 2
- sub_gain: bfloat16 [768], P(('dp', 'tp')), may hold values from 0.25 to 1.75
- sub_shift: bfloat16 [768], P(('dp', 'tp')), may hold values from -2 to 2
- ffn_gain: bfloat16 [768], P(('dp', 'tp')), may hold values from 0.25 to 1.75
- ffn_shift: bfloat16 [768], P(('dp', 'tp')), may hold values from -2 to 2
- fc1_weight: bfloat16 [3072, 768], P(('dp', 'tp')), may hold values from -0.21875 to 0.21875
- mid_gain: bfloat16 [3072], P(('dp', 'tp')), may hold values from 0.25 to 1.75
- mid_shift: bfloat16 [3072], P(('dp', 'tp')), may hold values from -2 to 2
- fc2_weight: bfloat16 [3072, 768], P(('dp', 'tp')), may hold values from -0.109375 to 0.109375
Outputs:
- block_out: bfloat16 [32768, 768], P(('dp', 'tp'))
- grad_tokens: bfloat16 [32768, 768], P(('dp', 'tp'))
- grad_qkv: float32 [768, 2304], P(('dp', 'tp'))
- grad_out: float32 [768, 768], P(('dp', 'tp'))
- grad_pre_gain: float32 [768], P(('dp', 'tp'))
- grad_pre_shift: float32 [768], P(('dp', 'tp'))
- grad_sub_gain: float32 [768], P(('dp', 'tp'))
- grad_sub_shift: float32 [768], P(('dp', 'tp'))
- grad_ffn_gain: float32 [768], P(('dp', 'tp'))
- grad_ffn_shift: float32 [768], P(('dp', 'tp'))
- grad_fc1: float32 [3072, 768], P(('dp', 'tp'))
- grad_mid_gain: float32 [3072], P(('dp', 'tp'))
- grad_mid_shift: float32 [3072], P(('dp', 'tp'))
- grad_fc2: float32 [3072, 768], P(('dp', 'tp'))
Inputs may be any that keep to these rules, and one draw needn't show every extreme that they name: `lengths`: each row lists one chip's sequences in the order they are packed; a row sums to 2048. Half of the chips, drawn from the seed, hold sequences of fewer than 512 tokens in which every two slots (0 and 1, 2 and 3, ...) sum to 512; the other half hold one sequence of more than 1024 tokens in slot 0, the rest of the rows in slot 1 (possibly 0), and zeros in the remaining slots.
All inputs are finite; a program needn't handle non-finite values.
Results may differ from a plain program's by a relative error of at most 0.012.
Values may be sent and summed in bfloat16 or wider, within the bound.
A program may use at most 192 MiB of HBM per device.

v0:
```python
import functools

import jax
import jax.numpy as jnp
import numpy as np
from jax import lax
from jax.experimental import pallas as pl
from jax.experimental.pallas import tpu as pltpu
from jax.sharding import PartitionSpec as P

f32, bf16 = jnp.float32, jnp.bfloat16
EPS = 1e-5
BIG = 1e30


def nt(a, b):
    return lax.dot_general(a, b, (((1,), (1,)), ((), ())), preferred_element_type=f32)


def nn(a, b):
    return lax.dot_general(a, b, (((1,), (0,)), ((), ())), preferred_element_type=f32)


def tn(a, b):
    return lax.dot_general(a, b, (((0,), (0,)), ((), ())), preferred_element_type=f32)

def doc_features(len_ref, rows, fq, fk):
    lane = lax.broadcasted_iota(jnp.int32, (1, 128), 1)
    lo = jnp.zeros((1, 128), jnp.int32); hi = jnp.zeros((1, 128), jnp.int32)
    run = jnp.int32(0)
    for d in range(8):
        nxt = run + len_ref[0, d]
        lo = jnp.where(lane == d, run, lo); hi = jnp.where(lane == d, nxt, hi)
        run = nxt
    def body(r, _):
        place = lax.broadcasted_iota(jnp.int32, (256, 128), 0) + r * 256
        hit = (place >= lo) & (place < hi)
        sl = pl.ds(pl.multiple_of(r * 256, 256), 256)
        fq[sl, :] = jnp.where(hit, 1.0, 0.0).astype(bf16)
        fk[sl, :] = jnp.where(hit | (lane >= 8), 0.0, -BIG).astype(bf16)
        return 0
    lax.fori_loop(0, rows // 256, body, 0)

def fwd_t(len_ref, qkv, o_ref, lse_ref, fq, fk, q2, st_s, m_s, l_s, acc, *, B, pairs, variant):
    rows = qkv.shape[0]; nb = rows // B; W = pairs * 128
    doc_features(len_ref, rows, fq, fk)
    half = lax.broadcasted_iota(jnp.int32, (1, 128), 1) < 64
    causal = lax.broadcasted_iota(jnp.int32, (B, B), 0) <= lax.broadcasted_iota(jnp.int32, (B, B), 1)
    causal = jnp.concatenate([causal, causal], axis=1)
    for p in range(pairs):
        def qstep(i, _, p=p):
            qs = pl.ds(pl.multiple_of(i * B, B), B)
            q = qkv[qs, p * 128:(p + 1) * 128] * bf16(0.125)
            fqb = fq[qs, :]
            z = jnp.zeros_like(q)
            q2[...] = jnp.concatenate([
                jnp.concatenate([jnp.where(half, q, z), fqb], axis=1),
                jnp.concatenate([jnp.where(half, z, q), fqb], axis=1)], axis=0)
            def score(j):
                ks = pl.ds(pl.multiple_of(j * B, B), B)
                k2 = jnp.concatenate([qkv[ks, W + p * 128:W + (p + 1) * 128], fk[ks, :]], axis=1)
                return nt(k2, q2[...])
            def vblk(j):
                ks = pl.ds(pl.multiple_of(j * B, B), B)
                return qkv[ks, 2 * W + p * 128:2 * W + (p + 1) * 128]
            if variant == "online":
                def block(j, masked, first):
                    s = score(j)
                    if masked: s = jnp.where(causal, s, -BIG)
                    mx = jnp.max(s, axis=0, keepdims=True)
                    if first: mn = mx
                    else:
                        mo = m_s[...]
                        mn = jnp.maximum(mo, mx); al = jnp.exp(mo - mn)
                    e = jnp.exp(s - mn)
                    su = jnp.sum(e, axis=0, keepdims=True)
                    pv = tn(vblk(j), e.astype(bf16))
                    if first: l_s[...] = su; acc[...] = pv
                    else: l_s[...] = l_s[...] * al + su; acc[...] = acc[...] * al + pv
                    m_s[...] = mn
                block(i, True, True)
                def kstep(j, _):
                    block(j, False, False); return 0
                lax.fori_loop(0, i, kstep, 0)
                m = m_s[...]; l = l_s[...]
            else:
                def part(s): return jnp.max(s.reshape(B // 8, 8, 2 * B), axis=0)
                s = jnp.where(causal, score(i), -BIG)
                st_s[i] = s
                def pass1(j, m8):
                    s = score(j); st_s[j] = s
                    return jnp.maximum(m8, part(s))
                m8 = lax.fori_loop(0, i, pass1, part(s))
                m = jnp.max(m8, axis=0, keepdims=True)
                acc[...] = jnp.zeros_like(acc)
                def pass2(j, l8):
                    e = jnp.exp(st_s[j] - m)
                    acc[...] += tn(vblk(j), e.astype(bf16))
                    return l8 + jnp.sum(e.reshape(B // 8, 8, 2 * B), axis=0)
                l8 = lax.fori_loop(0, i + 1, pass2, jnp.zeros((8, 2 * B), f32))
                l = jnp.sum(l8, axis=0, keepdims=True)
            r = 1.0 / l
            a = acc[...] * r
            ot = jnp.concatenate([a[:64, :B], a[64:, B:]], axis=0)
            o_ref[qs, p * 128:(p + 1) * 128] = ot.T.astype(o_ref.dtype)
            lse = m + jnp.log(l)
            lse_ref[2 * p:2 * p + 1, qs] = lse[:, :B]
            lse_ref[2 * p + 1:2 * p + 2, qs] = lse[:, B:]
            return 0
        lax.fori_loop(0, nb, qstep, 0)

def attn_fwd(lengths, qkv, B=256, variant="online"):
    rows, w3 = qkv.shape; W = w3 // 3; pairs = W // 128; nb = rows // B
    return pl.pallas_call(functools.partial(fwd_t, B=B, pairs=pairs, variant=variant), name="attn_fwd",
        out_shape=(jax.ShapeDtypeStruct((rows, W), bf16), jax.ShapeDtypeStruct((8, rows), f32)),
        in_specs=[pl.BlockSpec(memory_space=pltpu.SMEM), pl.BlockSpec(memory_space=pltpu.VMEM)],
        out_specs=(pl.BlockSpec(memory_space=pltpu.VMEM),) * 2,
        scratch_shapes=[pltpu.VMEM((rows, 128), bf16), pltpu.VMEM((rows, 128), bf16), pltpu.VMEM((2 * B, 256), bf16),
                        pltpu.VMEM((nb if variant != "online" else 1, B, 2 * B), f32),
                        pltpu.VMEM((1, 2 * B), f32), pltpu.VMEM((1, 2 * B), f32), pltpu.VMEM((128, 2 * B), f32)],
        compiler_params=pltpu.CompilerParams(vmem_limit_bytes=56 << 20))(lengths, qkv)

def bwd_kernel(len_ref, qkv, do_ref, lse_ref, dl_ref, out, fq, fk, q2, do2, dq, dk, dv, *, B, pairs, mode):
    rows = qkv.shape[0]; nb = rows // B; W = pairs * 128
    doc_features(len_ref, rows, fq, fk)
    half = lax.broadcasted_iota(jnp.int32, (1, 128), 1) < 64
    causal = lax.broadcasted_iota(jnp.int32, (B, B), 0) <= lax.broadcasted_iota(jnp.int32, (B, B), 1)
    causal = jnp.concatenate([causal, causal], axis=1)
    for p in range(pairs):
        def prep(i, _, p=p):
            qs = pl.ds(pl.multiple_of(i * B, B), B)
            q = qkv[qs, p * 128:(p + 1) * 128] * bf16(0.125)
            d = do_ref[qs, p * 128:(p + 1) * 128]
            fqb = fq[qs, :]
            z = jnp.zeros_like(q)
            q2[i] = jnp.concatenate([
                jnp.concatenate([jnp.where(half, q, z), fqb], axis=1),
                jnp.concatenate([jnp.where(half, z, q), fqb], axis=1)], axis=0)
            do2[i] = jnp.concatenate([jnp.where(half, d, z), jnp.where(half, z, d)], axis=0)
            dq[i] = jnp.zeros(dq.shape[1:], f32)
            return 0
        lax.fori_loop(0, nb, prep, 0)
        def kstep(j, _, p=p):
            ks = pl.ds(pl.multiple_of(j * B, B), B)
            kt = qkv[ks, W + p * 128:W + (p + 1) * 128]
            v = qkv[ks, 2 * W + p * 128:2 * W + (p + 1) * 128]
            k2 = jnp.concatenate([kt, fk[ks, :]], axis=1)
            def block(i, masked, first):
                qs = pl.ds(pl.multiple_of(i * B, B), B)
                lse = jnp.concatenate([lse_ref[2 * p:2 * p + 1, qs], lse_ref[2 * p + 1:2 * p + 2, qs]], axis=1)
                dl = jnp.concatenate([dl_ref[2 * p:2 * p + 1, qs], dl_ref[2 * p + 1:2 * p + 2, qs]], axis=1)
                qq = q2[i]; dd = do2[i]
                st = nt(k2, qq)
                pt = jnp.exp(st - lse)
                if masked: pt = jnp.where(causal, pt, 0.0)
                dp = nt(v, dd)
                ds = (pt * (dp - dl)).astype(bf16)
                dvp = nn(pt.astype(bf16), dd)
                dkp = nn(ds, qq[:, :128])
                if first: dv[...] = dvp; dk[...] = dkp
                else: dv[...] += dvp; dk[...] += dkp
                if mode == "tn":
                    dq[i] += tn(ds, kt)
                else:
                    dq[i] += tn(kt, ds)
            block(j, True, True)
            def qstep(i, _):
                block(i, False, False); return 0
            lax.fori_loop(j + 1, nb, qstep, 0)
            out[ks, W + p * 128:W + (p + 1) * 128] = dk[...].astype(bf16)
            out[ks, 2 * W + p * 128:2 * W + (p + 1) * 128] = dv[...].astype(bf16)
            return 0
        lax.fori_loop(0, nb, kstep, 0)
        def fin(i, _, p=p):
            qs = pl.ds(pl.multiple_of(i * B, B), B)
            if mode == "tn":
                d = dq[i]
                r = jnp.where(half, d[:B], d[B:])
            else:
                d = dq[i]
                r = jnp.concatenate([d[:64, :B], d[64:, B:]], axis=0).T
            out[qs, p * 128:(p + 1) * 128] = (r * 0.125).astype(bf16)
            return 0
        lax.fori_loop(0, nb, fin, 0)

def attn_bwd(lengths, qkv, do, lse, dl, B=256, mode="tn"):
    rows, w3 = qkv.shape; W = w3 // 3; pairs = W // 128; nb = rows // B
    dqs = (nb, 2 * B, 128) if mode == "tn" else (nb, 128, 2 * B)
    return pl.pallas_call(functools.partial(bwd_kernel, B=B, pairs=pairs, mode=mode), name="attn_bwd",
        out_shape=jax.ShapeDtypeStruct((rows, w3), bf16),
        in_specs=[pl.BlockSpec(memory_space=pltpu.SMEM)] + [pl.BlockSpec(memory_space=pltpu.VMEM)] * 4,
        out_specs=pl.BlockSpec(memory_space=pltpu.VMEM),
        scratch_shapes=[pltpu.VMEM((rows, 128), bf16), pltpu.VMEM((rows, 128), bf16), pltpu.VMEM((nb, 2 * B, 256), bf16),
                        pltpu.VMEM((nb, 2 * B, 128), bf16), pltpu.VMEM(dqs, f32), pltpu.VMEM((B, 128), f32), pltpu.VMEM((B, 128), f32)],
        compiler_params=pltpu.CompilerParams(vmem_limit_bytes=56 << 20))(lengths, qkv, do, lse, dl)

def stats(v):
    n = v.shape[-1]
    m = jnp.sum(v, axis=-1, keepdims=True) * (1.0 / n)
    c = v - m
    s = jnp.sum(c * c, axis=-1, keepdims=True) * (1.0 / n)
    r = lax.rsqrt(s + EPS)
    return c * r, r
def ln_back(w, vh, r, g):
    n = vh.shape[-1]
    wg = w * g
    a = jnp.sum(wg, axis=-1, keepdims=True) * (1.0 / n)
    b = jnp.sum(wg * vh, axis=-1, keepdims=True) * (1.0 / n)
    return r * (wg - a - vh * b)
def colsum(v): return jnp.sum(v, axis=0, keepdims=True)


def gelu_parts(h):
    return 0.5 + 0.5 * lax.erf(h * 0.7071067811865476), jnp.exp2(h * h * -0.7213475204444817) * 0.3989422804014327

def ffn_kernel(vec, mid, sel, o_h, x_h, g_h, wo_h, fc1_h, fc2_h,
               delta_ref, gvec, gmid, gfc1, gfc2, out_ref, dy_h, do_h, gwo_h,
               o_ref, x_ref, g_ref, wo, fc1, fc2, dy_ref, do_ref, gwo,
               h_s, u_s, d_s, dm_s, m_s, dh_s, c_s, b_s, y_s, dc_s, st_s, ws, *, T, NT, NC, SR, UT):
    step = pl.program_id(0)
    rows = x_ref.shape[0]
    ff, D = fc1.shape
    K = ff // NC
    NS = NT // UT
    ins = [pltpu.make_async_copy(h, v, ws.at[k]) for k, (h, v) in enumerate(
        ((o_h, o_ref), (wo_h, wo), (x_h, x_ref), (fc1_h, fc1), (g_h, g_ref), (fc2_h, fc2)))]
    outs = [pltpu.make_async_copy(v, h, ws.at[6 + k]) for k, (h, v) in enumerate(
        ((dy_h, dy_ref), (do_h, do_ref), (gwo_h, gwo)))]
    sg, sb, fg, fb = [vec[k:k + 1, :] for k in range(2, 6)]
    tiles = [slice(t * T, (t + 1) * T) for t in range(NT)]
    subs = [slice(r * SR, (r + 1) * SR) for r in range(T // SR)]
    cols = [slice(c * K, (c + 1) * K) for c in range(NC)]
    def fold(v):
        r = v[:, :128]
        for k in range(1, v.shape[1] // 128): r = r + v[:, k * 128:(k + 1) * 128]
        return r
    @pl.when(step == 0)
    def _():
        for l in ins: l.start()
        gvec[...] = jnp.zeros_like(gvec); gmid[...] = jnp.zeros_like(gmid)
        ins[0].wait(); ins[1].wait(); ins[2].wait()
        bs = []
        for sl in tiles:
            oh, _r = stats(o_ref[sl, :].astype(f32))
            b_s[sl, :] = (oh * sg + sb).astype(bf16)
        for sl in tiles:
            y_s[sl, :] = x_ref[sl, :].astype(f32) + nn(b_s[sl, :], wo[...])
        for sl in tiles:
            yh, _r = stats(y_s[sl, :])
            c_s[sl, :] = (yh * fg + fb).astype(bf16)
        ins[3].wait()
    base = jnp.minimum(step, NS - 1) * T
    rs = pl.ds(pl.multiple_of(base, T), T)
    sub_rows = lambda s: pl.ds(pl.multiple_of(base + s.start, SR), SR)
    total = lambda k: jnp.sum(jnp.sum(st_s[k], axis=0), axis=1, keepdims=True) * (1.0 / ff)
    def moments():
        mu = total(0)
        return mu, lax.rsqrt(total(1) - mu * mu + EPS)
    @pl.when(step < NS)
    def _():
        h_s[0] = nt(c_s[rs, :], fc1[cols[0], :])
        for c in range(NC):
            for s in subs:
                h = h_s[c % 2, s, :]
                phi, den = gelu_parts(h)
                u = h * phi
                u_s[s, cols[c]] = u
                d_s[s, cols[c]] = phi + h * den
                st_s[0, c, s, :] = fold(u); st_s[1, c, s, :] = fold(u * u)
            if c + 1 < NC: h_s[(c + 1) % 2] = nt(c_s[rs, :], fc1[cols[c + 1], :])
    @pl.when(step == 0)
    def _():
        ins[4].wait(); ins[5].wait()
    @pl.when(step < NS)
    def _():
        mu, R = moments()
        dm_s[:, cols[0]] = nt(g_ref[rs, :], fc2[cols[0], :])
        for c in range(NC):
            gain = mid[0:1, cols[c]]; shift = mid[1:2, cols[c]]
            g6 = jnp.zeros((8, K), f32); g7 = jnp.zeros((8, K), f32)
            for s in subs:
                uh = (u_s[s, cols[c]] - mu[s]) * R[s]
                u_s[s, cols[c]] = uh
                m_s[sub_rows(s), cols[c]] = (uh * gain + shift).astype(bf16)
                dm = dm_s[s, cols[c]]
                e = dm * gain
                dm_s[s, cols[c]] = e
                q = dm * uh
                g6 += jnp.sum(q.reshape(SR // 8, 8, K), axis=0); g7 += jnp.sum(dm.reshape(SR // 8, 8, K), axis=0)
                st_s[2, c, s, :] = fold(e); st_s[3, c, s, :] = fold(e * uh)
            gmid[6:7, cols[c]] += colsum(g6)
            gmid[7:8, cols[c]] += colsum(g7)
            if c + 1 < NC: dm_s[:, cols[c + 1]] = nt(g_ref[rs, :], fc2[cols[c + 1], :])
    @pl.when(step < NS)
    def _():
        R = moments()[1]
        se = total(2); seu = total(3)
        for c in range(NC):
            for s in subs:
                dh = (dm_s[s, cols[c]] - se[s] - u_s[s, cols[c]] * seu[s]) * R[s] * d_s[s, cols[c]]
                dh_s[sub_rows(s), cols[c]] = dh.astype(bf16)
            if c == 0:
                out_ref[rs, :] = (y_s[rs, :] + nn(m_s[rs, :], fc2[...])).astype(bf16)
    @pl.when(step < NS)
    def _():
        dc_s[rs, :] = nn(dh_s[rs, :], fc1[...])
    def grads(lanes):
        gfc2[0] = tn(m_s[:, lanes], g_ref[...]).astype(bf16)
        gfc1[0] = tn(dh_s[:, lanes], c_s[...]).astype(bf16)
    @pl.when(step == NS)
    def _():
        hs = []
        for sl in tiles:
            yh, yr = stats(y_s[sl, :])
            dc = dc_s[sl, :]
            gvec[4:5, :] += colsum(dc * yh)
            gvec[5:6, :] += colsum(dc)
            dy_ref[sl, :] = (g_ref[sl, :].astype(f32) + ln_back(dc, yh, yr, fg)).astype(bf16)
        for sl in tiles:
            dc_s[sl, :] = nt(dy_ref[sl, :], wo[...])
        for sl in tiles:
            dbn = dc_s[sl, :]
            o = o_ref[sl, :].astype(f32)
            oh, orr = stats(o)
            gvec[2:3, :] += colsum(dbn * oh)
            gvec[3:4, :] += colsum(dbn)
            do = ln_back(dbn, oh, orr, sg).astype(bf16)
            do_ref[sl, :] = do
            pr = do.astype(f32) * o
            hi = pr.astype(bf16)
            lo = (pr - hi.astype(f32)).astype(bf16)
            delta_ref[:, sl] = nt(sel[...], hi) + nt(sel[...], lo)
        grads(cols[0])
        gwo[...] = tn(b_s[...], dy_ref[...]).astype(bf16)
        for c in outs: c.start()
    @pl.when(step > NS)
    def _():
        grads(pl.ds(pl.multiple_of((step - NS) * K, K), K))
    @pl.when(step == NS + NC - 1)
    def _():
        for c in outs: c.wait()

def ffn(o, x, g, wo, fc1, fc2, vec, mid, T=256, K=512, dt=f32, SR=16, UT=1):
    rows, D = x.shape; ff = fc1.shape[0]; NC = ff // K; NT = rows // T; NS = NT // UT
    head = np.arange(D)[None] // 64
    sel = jnp.asarray((np.arange(16)[:, None] == head // (D // 128) * 8 + head % (D // 128)).astype(np.float32), bf16)
    one = dict(pipeline_mode=pl.Buffered(1))
    full = lambda *s: pl.BlockSpec(s, lambda i: (0,) * len(s), **one)
    A = pl.BlockSpec(memory_space=pl.ANY)
    chunk = pl.BlockSpec((1, K, D), lambda s: (jnp.maximum(s - NS, 0), 0, 0))
    sds = jax.ShapeDtypeStruct
    M = pltpu.VMEM
    act = sds((rows, D), bf16)
    delta, gvec, gmid, g1, g2, out, dy, do, gwo = pl.pallas_call(functools.partial(ffn_kernel, T=T, NT=NT, NC=NC, SR=SR, UT=UT), name="ffn",
        grid=(NS + NC,),
        in_specs=[full(8, D), full(8, ff), full(16, D)] + [A] * 6,
        out_specs=[full(16, rows), full(8, D), full(8, ff), chunk, chunk, full(rows, D)] + [A] * 3,
        out_shape=[sds((16, rows), f32), sds((8, D), f32), sds((8, ff), f32), sds((NC, K, D), bf16), sds((NC, K, D), bf16),
                   act, act, act, sds((D, D), bf16)],
        scratch_shapes=[M((rows, D), bf16), M((D, D), bf16), M((rows, D), bf16)][:0] + [M((rows, D), bf16), M((rows, D), bf16), M((rows, D), bf16),
                        M((D, D), bf16), M((ff, D), bf16), M((ff, D), bf16), M((rows, D), bf16), M((rows, D), bf16), M((D, D), bf16),
                        M((2, T, K), f32), M((T, ff), f32), M((T, ff), f32), M((T, ff), f32),
                        M((rows, ff), bf16), M((rows, ff), bf16), M((rows, D), bf16), M((rows, D), bf16), M((rows, D), f32), M((rows, D), f32),
                        M((4, NC, T, 128), f32), pltpu.SemaphoreType.DMA((10,))],
        compiler_params=pltpu.CompilerParams(vmem_limit_bytes=63 << 20, dimension_semantics=("arbitrary",)))(
            vec, mid, sel, o, x, g, wo, fc1, fc2)
    return out, dy, do, delta, gwo, g1, g2, gvec, gmid

MESH = pl.DeviceIdType.MESH

def place():
    dp, tp = lax.axis_index("dp"), lax.axis_index("tp")
    q, z = dp % 4, dp // 4
    dx = 1 - 2 * (dp % 2)
    dy = 2 - 4 * ((dp // 2) % 2)
    a, b = (1 - tp) * dx + tp * dy, tp * dx + (1 - tp) * dy
    return dict(dp=dp, tp=tp, z=z, q=q, qa=q + a, qb=q + b, qab=q + a + b,
                a=(dp + a, tp), b=(dp + b, tp), peer=(dp, 1 - tp),
                zs=[((dp + 4 * k) % 16, tp) for k in (1, 2, 3)], zi=[(z + k) % 4 for k in (1, 2, 3)])

def enter(w):
    bar = pltpu.get_barrier_semaphore()
    for d in [w["a"], w["b"], w["peer"]] + w["zs"]:
        pl.semaphore_signal(bar, inc=1, device_id=d, device_id_type=MESH)
    pl.semaphore_wait(bar, 6)

class Copy:
    def __init__(self, ss, rs):
        self.ss, self.rs, self.n, self.all = ss, rs, 0, []
    def __call__(self, src, dst, dev):
        c = pltpu.make_async_remote_copy(src_ref=src, dst_ref=dst, send_sem=self.ss.at[self.n], recv_sem=self.rs.at[self.n],
                                         device_id=dev, device_id_type=MESH)
        self.n += 1
        self.all.append(c)
        return c

def go_all(cs):
    for c in cs: c.start()

def got(cs):
    for c in cs: c.wait_recv()

class Gather:
    def __init__(self, copy, w, src, slot, view, peer):
        q, qa, qb, qab = w["q"], w["qa"], w["qb"], w["qab"]
        own = slot(w["z"], q)
        far = [slot(z, q) for z in w["zi"]]
        self.z = [copy(src, own, d) for d in w["zs"]]
        self.a = [copy(src, own, w["a"])] + [copy(s, s, w["a"]) for s in far]
        self.b = [copy(src, own, w["b"])] + [copy(s, s, w["b"]) for s in far]
        self.ab = [copy(view(qa), view(qa), w["b"])]
        self.p = [copy(view(c), view(c), w["peer"]) for c in (q, qa, qb, qab)] if peer else []
    def start(self):
        go_all(self.z + self.a[:1] + self.b[:1])
    def after_z(self):
        got(self.z)
        for k in (1, 2, 3): go_all([self.a[k], self.b[k]])
        go_all(self.p[:1])
    def after_a(self):
        got(self.a)
        go_all(self.ab + self.p[1:2])
    def after_b(self):
        got(self.b + self.ab)
        go_all(self.p[2:])
    def finish(self):
        got(self.p)

N_COPIES = 112

def k12_kernel(len_ref, tok, wq, wos, vpk, e24, e96, rsel, fc1s, fc2s,
               o_out, lse_ref, vec, mid, xh_h, qkv_h, wown_h, wo_h, fc1_h, fc2_h,
               xh16, qkv, wown, afull, xp, vbuf, sb, rb, woc, o_loc, fq, fk, q2, m_s, l_s, acc, ss, rs, ls, *, B, pairs, stage=9):
    w = place()
    tp = w["tp"]
    rows, D = tok.shape
    W = pairs * 128
    send = Copy(ss, rs)
    first = tp == 0
    sb[...] = jnp.zeros_like(sb)
    pick = lambda c0, n: (jnp.where(first, wq[:, c0:c0 + W], wq[:, c0 + W:c0 + 2 * W]).astype(bf16),
                          jnp.where(first, wq[:, c0 + W:c0 + 2 * W], wq[:, c0:c0 + W]).astype(bf16))
    mine = []
    for k in range(3):
        own, oth = pick(k * D, W)
        mine.append(own); sb[0:24, k * W:(k + 1) * W] = oth
    own_o = jnp.where(first, wos[:, :W], wos[:, W:])
    sb[0:24, 3 * W:4 * W] = jnp.where(first, wos[:, W:], wos[:, :W])
    vbuf[w["z"], w["q"], tp] = vpk[...]
    loc = [pltpu.make_async_copy(fc1s, fc1_h.at[w["z"], w["q"], tp], ls.at[0]),
           pltpu.make_async_copy(fc2s, fc2_h.at[w["z"], w["q"], tp], ls.at[1])]
    for c in loc: c.start()
    enter(w)
    cpre = send(sb, rb, w["peer"])
    gv = Gather(send, w, vbuf.at[w["z"], w["q"], tp], lambda z, q: vbuf.at[z, q, tp], lambda q: vbuf.at[:, q, tp], True)
    cx = send(tok, xp, w["peer"])
    gq = [Gather(send, w, wown.at[p, w["z"], w["q"]], lambda z, q, p=p: wown.at[p, z, q], lambda q, p=p: wown.at[p, :, q], False)
          for p in range(pairs)]
    keep = [pltpu.make_async_copy(v, h, ls.at[3 + k]) for k, (v, h) in enumerate(((xh16, xh_h), (qkv, qkv_h), (wown, wown_h)))]
    cols = pl.ds(pl.multiple_of(tp * W, 128), W)
    go = Gather(send, w, woc, lambda z, q: wo_h.at[z, q, :, cols], lambda q: wo_h.at[:, q, :, cols], True)
    g1 = Gather(send, w, fc1s, lambda z, q: fc1_h.at[z, q, tp], lambda q: fc1_h.at[:, q, tp], True)
    g2 = Gather(send, w, fc2s, lambda z, q: fc2_h.at[z, q, tp], lambda q: fc2_h.at[:, q, tp], True)
    peer_rows = pl.ds(pl.multiple_of((1 - tp) * rows, rows), rows)
    co = [send(o_loc.at[peer_rows, p * 128:(p + 1) * 128],
               o_out.at[:, pl.ds(pl.multiple_of(tp * W + p * 128, 128), 128)], w["peer"]) for p in range(pairs)]
    cpre.start()
    gv.start()
    cx.start()
    cpre.wait_recv()
    other = rb[0:24, :].astype(f32)
    me = jnp.concatenate(mine + [own_o], axis=1).astype(f32)
    both = jnp.concatenate([jnp.where(first, me, other), jnp.where(first, other, me)], axis=0).astype(bf16)
    for p in range(pairs):
        for k in range(3):
            wown[p, w["z"], w["q"], :, k * 128:(k + 1) * 128] = both[:, k * W + p * 128:k * W + (p + 1) * 128]
    woc[...] = both[:, 3 * W:]
    gq[0].start()
    lw = pltpu.make_async_copy(woc, wo_h.at[w["z"], w["q"], :, cols], ls.at[2])
    lw.start()
    gv.after_z(); gv.after_a()
    gq[0].after_z()
    gq[1].start()
    gv.after_b(); gv.finish()
    small = nn(rsel[...], vbuf[...].reshape(512, 128)).astype(bf16)
    dev = lax.broadcasted_iota(jnp.int32, (32, 1), 0)
    def spread(v, e, n):
        lane = lax.broadcasted_iota(jnp.int32, (1, e.shape[1]), 1)
        hit = (lane >= dev * n) & (lane < dev * n + n)
        return colsum(jnp.where(hit, nn(small[v * 32:(v + 1) * 32], e[...]), 0.0))
    for v in range(2): vec[v:v + 1, :] = spread(v, e24, 24)
    gq[0].after_a()
    def normed(src, base):
        def body(r, _):
            sl = pl.ds(pl.multiple_of(r * 256, 256), 256)
            xh, _r = stats(src[sl, :].astype(f32))
            to = pl.ds(pl.multiple_of(base + r * 256, 256), 256)
            xh16[to, :] = xh.astype(bf16)
            afull[to, :] = (xh * vec[0:1, :] + vec[1:2, :]).astype(bf16)
            return 0
        lax.fori_loop(0, rows // 256, body, 0)
    normed(tok, tp * rows)
    gq[0].after_b()
    gq[1].after_z()
    gq[2].start()
    for c in loc: c.wait()
    lw.wait()
    go.start(); g1.start()
    cx.wait_recv()
    normed(xp, (1 - tp) * rows)
    keep[0].start()
    doc_features(len_ref, 2 * rows, fq, fk)
    def proj(p):
        def body(r, _):
            sl = pl.ds(pl.multiple_of(r * 512, 512), 512)
            qkv[sl, p * 3 * 128:(p + 1) * 3 * 128] = nn(afull[sl, :], wown[p].reshape(D, 3 * 128)).astype(bf16)
            return 0
        lax.fori_loop(0, 2 * rows // 512, body, 0)
    proj(0)
    gq[1].after_a(); gq[2].after_z()
    g2.start()
    for v in range(2, 6): vec[v:v + 1, :] = spread(v, e24, 24)
    vec[6:8, :] = jnp.zeros((2, D), f32)
    for v in range(2): mid[v:v + 1, :] = spread(6 + v, e96, 96)
    mid[2:8, :] = jnp.zeros((6, 4 * D), f32)
    nb = 2 * rows // B
    half = lax.broadcasted_iota(jnp.int32, (1, 128), 1) < 64
    causal = lax.broadcasted_iota(jnp.int32, (B, B), 0) <= lax.broadcasted_iota(jnp.int32, (B, B), 1)
    causal = jnp.concatenate([causal, causal], axis=1)
    def unit(u, _):
        p, i = u // nb, u % nb
        def at(k):
            def deco(f): pl.when(u == k)(f)
            return deco
        @at(1)
        def _():
            gq[1].after_b(); gq[2].after_a()
        @at(3)
        def _():
            gq[2].after_b()
            keep[2].start()
        @at(4)
        def _():
            co[0].start()
            go.after_z(); g1.after_z()
            proj(1)
        @at(6)
        def _():
            go.after_a(); g1.after_a(); g2.after_z()
        @at(7)
        def _():
            go.after_b()
        @at(8)
        def _():
            co[1].start()
            proj(2)
            keep[1].start()
            g1.after_b()
        @at(10)
        def _():
            g2.after_a()
        qs = pl.ds(pl.multiple_of(i * B, B), B)
        lanes = lambda k: pl.ds(pl.multiple_of(p * 384 + k * 128, 128), 128)
        q = qkv[qs, lanes(0)] * bf16(0.125)
        fqb = fq[qs, :]
        z = jnp.zeros_like(q)
        q2[...] = jnp.concatenate([
            jnp.concatenate([jnp.where(half, q, z), fqb], axis=1),
            jnp.concatenate([jnp.where(half, z, q), fqb], axis=1)], axis=0)
        def block(j, diag):
            ks = pl.ds(pl.multiple_of(j * B, B), B)
            s = nt(jnp.concatenate([qkv[ks, lanes(1)], fk[ks, :]], axis=1), q2[...])
            if diag: s = jnp.where(causal, s, -BIG)
            mn = jnp.max(s, axis=0, keepdims=True)
            if not diag:
                mo = m_s[...]
                mn = jnp.maximum(mo, mn); al = jnp.exp(mo - mn)
            e = jnp.exp(s - mn)
            su = jnp.sum(e, axis=0, keepdims=True)
            pv = tn(qkv[ks, lanes(2)], e.astype(bf16))
            if diag: l_s[...] = su; acc[...] = pv
            else: l_s[...] = l_s[...] * al + su; acc[...] = acc[...] * al + pv
            m_s[...] = mn
        block(i, True)
        def kstep(j, _):
            block(j, False); return 0
        lax.fori_loop(0, i, kstep, 0)
        l = l_s[...]
        a = acc[...] * (1.0 / l)
        ot = jnp.concatenate([a[:64, :B], a[64:, B:]], axis=0)
        o_loc[qs, pl.ds(pl.multiple_of(p * 128, 128), 128)] = ot.T.astype(bf16)
        lse = m_s[...] + jnp.log(l)
        lse_ref[p, 0:1, qs] = lse[:, :B]
        lse_ref[p, 1:2, qs] = lse[:, B:]
        return 0
    lax.fori_loop(0, pairs * nb, unit, 0)
    co[2].start()
    g2.after_b()
    o_out[:, cols] = o_loc[pl.ds(pl.multiple_of(tp * rows, rows), rows), :]
    got(co)
    go.finish(); g1.finish(); g2.finish()
    for c in send.all: c.wait_send()
    for c in keep: c.wait()

def consts_np(D):
    k = np.arange(128)[:, None]
    e24 = (np.arange(D)[None] % 24 == k).astype(np.float32)
    e96 = (np.arange(4 * D)[None] % 96 == k).astype(np.float32)
    r = np.arange(256)[:, None]
    rsel = (np.arange(512)[None] == (r % 32) * 16 + r // 32).astype(np.float32)
    return e24, e96, rsel

def consts(D):
    return [jnp.asarray(c, bf16) for c in consts_np(D)]

def k12(lengths, tok, wq, wos, vpk, fc1s, fc2s, B=512):
    rows, D = tok.shape
    W = D // 2; pairs = W // 128
    V, A = pl.BlockSpec(memory_space=pltpu.VMEM), pl.BlockSpec(memory_space=pl.ANY)
    sds = jax.ShapeDtypeStruct
    hid = fc1s.shape[0]
    return pl.pallas_call(functools.partial(k12_kernel, B=B, pairs=pairs), name="forward",
        out_shape=(sds((rows, D), bf16), sds((pairs, 2, 2 * rows), f32), sds((8, D), f32), sds((8, 4 * D), f32),
                   sds((2 * rows, D), bf16), sds((2 * rows, 3 * W), bf16), sds((pairs, 4, 4, 48, 3 * 128), bf16),
                   sds((4, 4, 48, D), bf16), sds((4, 4, 2, hid, D), bf16), sds((4, 4, 2, hid, D), bf16)),
        in_specs=[pl.BlockSpec(memory_space=pltpu.SMEM)] + [V] * 7 + [A] * 2,
        out_specs=(V,) * 4 + (A,) * 6,
        scratch_shapes=[pltpu.VMEM((2 * rows, D), bf16), pltpu.VMEM((2 * rows, 3 * W), bf16), pltpu.VMEM((pairs, 4, 4, 48, 3 * 128), bf16), pltpu.VMEM((2 * rows, D), bf16), pltpu.VMEM((rows, D), bf16), pltpu.VMEM((4, 4, 2, 16, 128), bf16), pltpu.VMEM((32, 4 * W), bf16), pltpu.VMEM((32, 4 * W), bf16),
                        pltpu.VMEM((48, W), bf16), pltpu.VMEM((2 * rows, W), bf16), pltpu.VMEM((2 * rows, 128), bf16), pltpu.VMEM((2 * rows, 128), bf16),
                        pltpu.VMEM((2 * B, 256), bf16), pltpu.VMEM((1, 2 * B), f32), pltpu.VMEM((1, 2 * B), f32), pltpu.VMEM((128, 2 * B), f32),
                        pltpu.SemaphoreType.DMA((N_COPIES,)), pltpu.SemaphoreType.DMA((N_COPIES,)), pltpu.SemaphoreType.DMA((6,))],
        compiler_params=pltpu.CompilerParams(vmem_limit_bytes=60 << 20, collective_id=0, has_side_effects=True))(
            lengths, tok, wq, wos, vpk, *consts(D), fc1s, fc2s)

def pack_vectors(six, two):
    n6 = jnp.pad(jnp.stack(six), ((0, 0), (0, 128 - six[0].shape[0])))
    n2 = jnp.pad(jnp.stack(two), ((0, 8), (0, 128 - two[0].shape[0])))
    return jnp.concatenate([n6, n2], axis=0)


def add(x, y):
    return (x.astype(f32) + y.astype(f32)).astype(x.dtype)

class Scatter:
    def __init__(self, copy, w, s, bb, ab, zb):
        self.w, self.s, self.bb, self.ab, self.zb = w, s, bb, ab, zb
        self.b = [copy(s.at[:, w["qb"]], bb.at[0], w["b"]), copy(s.at[:, w["qab"]], bb.at[1], w["b"])]
        self.a = [copy(s.at[:, w["qa"]], ab, w["a"])]
        self.z = [copy(s.at[w["zi"][k], w["q"]], zb.at[k], w["zs"][k]) for k in range(3)]
    def go(self, cs):
        for c in cs: c.start()
    def start(self):
        self.go(self.b)
    def after_b(self):
        for c in self.b: c.wait_recv()
        for z in range(4):
            self.s[z, self.w["qa"]] = add(self.s[z, self.w["qa"]], self.bb[1, z])
        self.go(self.a)
        for z in range(4):
            self.s[z, self.w["q"]] = add(self.s[z, self.w["q"]], self.bb[0, z])
    def after_a(self):
        for c in self.a: c.wait_recv()
        for z in range(4):
            self.s[z, self.w["q"]] = add(self.s[z, self.w["q"]], self.ab[z])
        self.go(self.z)
    def result(self):
        for c in self.z: c.wait_recv()
        r = self.s[self.w["z"], self.w["q"]].astype(f32)
        for k in range(3): r = r + self.zb[k].astype(f32)
        return r

def k45_kernel(len_ref, do, delta, lse_ref, vec, gvec, gmid, e24t, e96t, qkv_h, xh_h, wown_h, gwo_h, tok_h, dy_h, g1_h, g2_h,
               gtok, gq_o, gwo_o, g1_o, g2_o, small_o, pre_o,
               qkv, xh16, wown, gwo, tok, dy, do_own, dl_own, fq, fk, q2, do2, dq, dk, dv,
               s1, r1, b1, a1, z1, s2, r2, b2, a2, z2, so, ro, bo, ao, zo, *rest, B, pairs):
    flows, rest = rest[:4 * pairs], rest[4 * pairs:]
    (sm, pm, s4, bm, am, zm, da, dsend, drecv, fo, xo, fqk, xq, gcol, bcol, vacc, uacc, ss, rs, ls) = rest
    w = place()
    tp = w["tp"]
    rows, D = tok.shape
    W = pairs * 128
    nb = 2 * rows // B
    first = tp == 0
    other = 1 - tp
    mine_rows = pl.ds(pl.multiple_of(tp * rows, rows), rows)
    mine_cols = pl.ds(pl.multiple_of(tp * W, 128), W)
    other_cols = pl.ds(pl.multiple_of(other * W, 128), W)
    copy = Copy(ss, rs)
    c_do = copy(do.at[:, other_cols], do_own.at[mine_rows, :], w["peer"])
    c_dl = copy(delta.at[pl.ds(pl.multiple_of(other * 8, 8), 8), :], dl_own.at[:, mine_rows], w["peer"])
    c_r2 = copy(g2_h.at[:, :, other], r2, w["peer"])
    c_r1 = copy(g1_h.at[:, :, other], r1, w["peer"])
    c_ro = copy(gwo_h.at[:, other_cols], ro, w["peer"])
    f1, f2 = Scatter(copy, w, s1, b1, a1, z1), Scatter(copy, w, s2, b2, a2, z2)
    fo_ = Scatter(copy, w, so, bo, ao, zo)
    fqs = [Scatter(copy, w, *flows[4 * p:4 * p + 4]) for p in range(pairs)]
    fm = Scatter(copy, w, s4, bm, am, zm)
    c_pm = copy(sm.at[:, :, other], pm, w["peer"])
    hr = rows // 2
    c_da = [copy(dsend.at[pl.ds(k * hr, hr), :], drecv.at[pl.ds(k * hr, hr), :], w["peer"]) for k in range(2)]
    n = gq_o.shape[0]
    other_n = pl.ds(pl.multiple_of(other * n, 8), n)
    mine_n = pl.ds(pl.multiple_of(tp * n, 8), n)
    c_xo = copy(fo.at[other_n, :], xo, w["peer"])
    c_xq = copy(fqk.at[other_n, :], xq, w["peer"])
    l_q = pltpu.make_async_copy(qkv_h, qkv, ls.at[0])
    l_2 = pltpu.make_async_copy(g2_h.at[:, :, tp], s2, ls.at[1])
    l_1 = pltpu.make_async_copy(g1_h.at[:, :, tp], s1, ls.at[2])
    l_t = pltpu.make_async_copy(tok_h, tok, ls.at[3])
    l_y = pltpu.make_async_copy(dy_h, dy, ls.at[4])
    l_o = pltpu.make_async_copy(gwo_h, gwo, ls.at[5])
    l_x = pltpu.make_async_copy(xh_h, xh16, ls.at[6])
    l_w = [pltpu.make_async_copy(wown_h.at[p], wown.at[:, p * 384:(p + 1) * 384], ls.at[7 + p]) for p in range(pairs)]
    for l in [l_q, l_2, l_o, l_1, l_x] + l_w + [l_t, l_y]: l.start()
    enter(w)
    for c in (c_do, c_dl, c_ro, c_r2, c_r1): c.start()
    do_own[mine_rows, :] = do[:, mine_cols]
    dl_own[:, mine_rows] = delta[pl.ds(pl.multiple_of(tp * 8, 8), 8), :]
    doc_features(len_ref, 2 * rows, fq, fk)
    dev = lax.broadcasted_iota(jnp.int32, (32, 1, 1), 0)
    def pieces(v, e, n):
        lane = lax.broadcasted_iota(jnp.int32, (1, 1, v.shape[1]), 2)
        hit = (lane >= dev * n) & (lane < dev * n + n)
        t = jnp.where(hit, v[None], 0.0).reshape(256, v.shape[1])
        hi = t.astype(bf16)
        return nn(hi, e) + nn((t - hi.astype(f32)).astype(bf16), e)
    early = pieces(gmid[...], e96t[...], 4 * D // 32) + pieces(gvec[...], e24t[...], D // 32)
    sm[...] = early.reshape(4, 4, 2, 8, 128)
    c_pm.start()
    gcol[...] = jnp.broadcast_to(vec[0:1, :], (128, D)).T
    bcol[...] = jnp.broadcast_to(vec[1:2, :], (128, D)).T
    vacc[...] = jnp.zeros_like(vacc); uacc[...] = jnp.zeros_like(uacc)
    l_q.wait()
    c_do.wait_recv(); c_dl.wait_recv()

    half = lax.broadcasted_iota(jnp.int32, (1, 128), 1) < 64
    causal = lax.broadcasted_iota(jnp.int32, (B, B), 0) <= lax.broadcasted_iota(jnp.int32, (B, B), 1)
    causal = jnp.concatenate([causal, causal], axis=1)
    def grads(p):
        out = flows[4 * p]
        cs = [slice(p * 384 + k * 128, p * 384 + (k + 1) * 128) for k in range(3)]
        g = qkv[:, p * 384:(p + 1) * 384]
        t = tn(xh16[...], g)
        gsum = jnp.sum(g.astype(f32), axis=0, keepdims=True)
        for k in range(3):
            sl = slice(k * 128, (k + 1) * 128)
            wk = wown[:, cs[k]].astype(f32)
            tk, sk = t[:, sl], gsum[:, sl]
            out[:, :, :, sl] = (gcol[...] * tk + bcol[...] * sk).astype(bf16).reshape(4, 4, 48, 128)
            vacc[...] += tk * wk
            uacc[...] += sk * wk
        if p == pairs - 1:
            lane = lax.broadcasted_iota(jnp.int32, (1, 128), 1)
            e = jnp.where(lane == 0, jnp.sum(vacc[...], axis=1, keepdims=True), 0.0)
            e = jnp.where(lane == 1, jnp.sum(uacc[...], axis=1, keepdims=True), e)
            out[:, :, :, 384:512] = e.astype(bf16).reshape(4, 4, 48, 128)
    def unit(u, _):
        p, j = u // nb, u % nb
        lanes = lambda k: pl.ds(pl.multiple_of(p * 384 + k * 128, 128), 128)
        def at(k):
            def deco(f): pl.when(u == k)(f)
            return deco
        @at(1)
        def _():
            c_pm.wait_recv()
            for z in range(4):
                for k in range(4): s4[z, k] = sm[z, k, tp] + pm[z, k]
            fm.start()
            c_r2.wait_recv(); l_2.wait()
            for z in range(4):
                for k in range(4): s2[z, k] = add(s2[z, k], r2[z, k])
            f2.start()
            c_ro.wait_recv(); l_o.wait()
            so[...] = add(gwo[:, mine_cols], ro[...]).reshape(so.shape)
            fo_.start()
        @at(2)
        def _():
            fm.after_b()
            c_r1.wait_recv(); l_1.wait()
            for z in range(4):
                for k in range(4): s1[z, k] = add(s1[z, k], r1[z, k])
            f1.start()
        @at(3)
        def _():
            fm.after_a()
        @at(4)
        def _():
            l_x.wait()
            for l in l_w: l.wait()
            grads(0)
            f2.after_b(); fo_.after_b(); fqs[0].start()
            small_o[...] = fm.result()
        @at(5)
        def _():
            f2.after_a(); fo_.after_a()
        @at(6)
        def _():
            f1.after_b(); fqs[0].after_b()
        @at(7)
        def _():
            fqs[0].after_a()
        @at(8)
        def _():
            f1.after_a(); grads(1); fqs[1].start()
            g2_o[...] = f2.result()
            fo[...] = fo_.result()
            c_xo.start()
        @at(9)
        def _():
            fqs[1].after_b()
        @at(10)
        def _():
            fqs[1].after_a()
        @pl.when(j == 0)
        def _():
            def prep(i, _):
                qs = pl.ds(pl.multiple_of(i * B, B), B)
                q = qkv[qs, lanes(0)] * bf16(0.125)
                d = do_own[qs, pl.ds(pl.multiple_of(p * 128, 128), 128)]
                fqb = fq[qs, :]
                z = jnp.zeros_like(q)
                q2[i] = jnp.concatenate([
                    jnp.concatenate([jnp.where(half, q, z), fqb], axis=1),
                    jnp.concatenate([jnp.where(half, z, q), fqb], axis=1)], axis=0)
                do2[i] = jnp.concatenate([jnp.where(half, d, z), jnp.where(half, z, d)], axis=0)
                dq[i] = jnp.zeros(dq.shape[1:], f32)
                return 0
            lax.fori_loop(0, nb, prep, 0)
        ks = pl.ds(pl.multiple_of(j * B, B), B)
        kt = qkv[ks, lanes(1)]
        v = qkv[ks, lanes(2)]
        k2 = jnp.concatenate([kt, fk[ks, :]], axis=1)
        def block(i, diag):
            qs = pl.ds(pl.multiple_of(i * B, B), B)
            lse = jnp.concatenate([lse_ref[p, 0:1, qs], lse_ref[p, 1:2, qs]], axis=1)
            d0 = pl.ds(2 * p, 1); d1 = pl.ds(2 * p + 1, 1)
            dl = jnp.concatenate([dl_own[d0, qs], dl_own[d1, qs]], axis=1)
            qq = q2[i]; dd = do2[i]
            pt = jnp.exp(nt(k2, qq) - lse)
            if diag: pt = jnp.where(causal, pt, 0.0)
            ds = (pt * (nt(v, dd) - dl)).astype(bf16)
            dvp = nn(pt.astype(bf16), dd)
            dkp = nn(ds, qq[:, :128])
            if diag: dv[...] = dvp; dk[...] = dkp
            else: dv[...] += dvp; dk[...] += dkp
            dq[i] += tn(ds, kt)
        block(j, True)
        def qstep(i, _):
            block(i, False); return 0
        lax.fori_loop(j + 1, nb, qstep, 0)
        qkv[ks, lanes(1)] = dk[...].astype(bf16)
        qkv[ks, lanes(2)] = dv[...].astype(bf16)
        @pl.when(j == nb - 1)
        def _():
            def fin(i, _):
                qs = pl.ds(pl.multiple_of(i * B, B), B)
                d = dq[i]
                qkv[qs, lanes(0)] = (jnp.where(half, d[:B], d[B:]) * 0.125).astype(bf16)
                return 0
            lax.fori_loop(0, nb, fin, 0)
        return 0
    lax.fori_loop(0, pairs * nb, unit, 0)
    grads(2)
    fqs[2].start()
    for k in range(2):
        sl = pl.ds(pl.multiple_of(other * rows + k * hr, hr), hr)
        dsend[k * hr:(k + 1) * hr, :] = nt(qkv[sl, :], wown[...]).astype(bf16)
        c_da[k].start()
    fqs[2].after_b()
    g1_o[...] = f1.result()
    for k in range(2):
        sl = pl.ds(pl.multiple_of(tp * rows + k * hr, hr), hr)
        da[k * hr:(k + 1) * hr, :] = nt(qkv[sl, :], wown[...])
        if k == 0: fqs[2].after_a()
    l_t.wait(); l_y.wait()
    for c in c_da: c.wait_recv()
    gain = vec[0:1, :]
    def fin(r, _):
        sl = pl.ds(pl.multiple_of(r * 256, 256), 256)
        d = da[sl, :] + drecv[sl, :].astype(f32)
        xh, xr = stats(tok[sl, :].astype(f32))
        gtok[sl, :] = (dy[sl, :].astype(f32) + ln_back(d, xh, xr, gain)).astype(bf16)
        return 0
    def collect(p):
        r = fqs[p].result()
        fqk[:, p * 384:(p + 1) * 384] = r[:, :384]
        if p == pairs - 1: fqk[:, pairs * 384:] = r[:, 384:]
    for p in range(pairs - 1): collect(p)
    lax.fori_loop(0, rows // 256, fin, 0)
    collect(pairs - 1)
    c_xq.start()
    c_xo.wait_recv()
    mine = fo[mine_n, :]
    gwo_o[:, :W] = jnp.where(first, mine, xo[...])
    gwo_o[:, W:] = jnp.where(first, xo[...], mine)
    c_xq.wait_recv()
    for p in range(pairs):
        for k in range(3):
            src = p * 384 + k * 128
            mine = fqk[mine_n, src:src + 128]
            oth = xq[:, src:src + 128]
            c0 = k * D + p * 128
            gq_o[:, c0:c0 + 128] = jnp.where(first, mine, oth)
            gq_o[:, c0 + W:c0 + W + 128] = jnp.where(first, oth, mine)
    pre_o[...] = fqk[mine_n, 3 * W:] + xq[:, 3 * W:]
    for c in copy.all: c.wait_send()

def k45(lengths, xh, wown, do, delta, lse, vec, gvec, gmid, gwo, qkv, tok, dy, g1, g2, B=512):
    rows, D = tok.shape
    W = D // 2; pairs = W // 128; nb = 2 * rows // B
    V, A = pl.BlockSpec(memory_space=pltpu.VMEM), pl.BlockSpec(memory_space=pl.ANY)
    sds = jax.ShapeDtypeStruct
    hid = g1.shape[3]
    M = pltpu.VMEM
    e24t, e96t = [c.T for c in consts_np(D)[:2]]
    def flow(r, c, t, lead=()):
        return [M(lead + (4, 4, r, c), t), M(lead + (2, 4, r, c), t), M(lead + (4, r, c), t), M(lead + (3, r, c), t)]
    fc = flow(hid, D, bf16)
    fc = [fc[0], M((4, 4, hid, D), bf16)] + fc[1:]
    wo = flow(48, W, bf16)
    wo = [wo[0], M((D, W), bf16)] + wo[1:]
    sm = flow(8, 128, f32)
    return pl.pallas_call(functools.partial(k45_kernel, B=B, pairs=pairs), name="backward",
        out_shape=(sds((rows, D), bf16), sds((D // 32, 3 * D), f32), sds((D // 32, D), f32), sds((hid, D), f32), sds((hid, D), f32), sds((8, 128), f32), sds((D // 32, 128), f32)),
        in_specs=[pl.BlockSpec(memory_space=pltpu.SMEM)] + [V] * 8 + [A] * 8,
        out_specs=(V,) * 7,
        scratch_shapes=[M((2 * rows, 3 * W), bf16), M((2 * rows, D), bf16), M((D, 3 * W), bf16), M((D, D), bf16), M((rows, D), bf16), M((rows, D), dy.dtype), M((2 * rows, W), bf16), M((8, 2 * rows), f32),
                        M((2 * rows, 128), bf16), M((2 * rows, 128), bf16), M((nb, 2 * B, 256), bf16), M((nb, 2 * B, 128), bf16), M((nb, 2 * B, 128), f32),
                        M((B, 128), f32), M((B, 128), f32)] + fc + fc + wo + flow(48, W, bf16) * (pairs - 1) + flow(48, W + 128, bf16) +
                       [M((4, 4, 2, 8, 128), f32), M((4, 4, 8, 128), f32)] + sm +
                       [M((rows, D), f32), M((rows, D), bf16), M((rows, D), bf16), M((48, W), f32), M((24, W), f32), M((48, 3 * W + 128), f32), M((24, 3 * W + 128), f32),
                        M((D, 128), f32), M((D, 128), f32), M((D, 128), f32), M((D, 128), f32),
                        pltpu.SemaphoreType.DMA((64,)), pltpu.SemaphoreType.DMA((64,)), pltpu.SemaphoreType.DMA((10,))],
        compiler_params=pltpu.CompilerParams(vmem_limit_bytes=63 << 20, collective_id=1, has_side_effects=True))(
            lengths, do, delta, lse, vec, gvec, gmid, jnp.asarray(e24t, bf16), jnp.asarray(e96t, bf16), qkv, xh, wown, gwo, tok, dy, g1, g2)

def local_fast(tokens, cotangent, lengths, qkv_weight, out_weight, pre_gain, pre_shift, sub_gain, sub_shift,
          ffn_gain, ffn_shift, fc1_weight, mid_gain, mid_shift, fc2_weight):
    rows, D = tokens.shape
    vpk = pack_vectors([pre_gain, pre_shift, sub_gain, sub_shift, ffn_gain, ffn_shift], [mid_gain, mid_shift])
    o, lse, vec, mid, xh16, qkv, wown, wo, fc1, fc2 = k12(lengths, tokens, qkv_weight, out_weight, vpk, fc1_weight, fc2_weight)
    block_out, dy, do, delta, gwo, g1, g2, gvec, gmid = ffn(o, tokens, cotangent, wo.reshape(D, D), fc1.reshape(4 * D, D), fc2.reshape(4 * D, D), vec, mid)
    shape = (4, 4, 2, fc1_weight.shape[0], D)
    gtok, gq, gwo, g1, g2, small, pre = k45(lengths, xh16, wown.reshape(3, D, 384), do, delta, lse, vec, gvec, gmid, gwo, qkv, tokens, dy, g1.reshape(shape), g2.reshape(shape))
    n, m = pre_gain.shape[0], mid_gain.shape[0]
    return (block_out, gtok, gq, gwo, pre[:, 0], pre[:, 1], small[2, :n], small[3, :n], small[4, :n], small[5, :n],
            g1, small[6, :m], small[7, :m], g2)

def norm(v):
    return stats(v)


def local_any(tokens, cotangent, lengths, qkv_weight, out_weight, pre_gain, pre_shift, sub_gain, sub_shift,
          ffn_gain, ffn_shift, fc1_weight, mid_gain, mid_shift, fc2_weight):
    rows, D = tokens.shape
    W = D // 2
    tp = lax.axis_index("tp")
    both = ("dp", "tp")
    gather = lambda a: lax.all_gather(a, both, axis=0, tiled=True)
    small = gather(jnp.stack([pre_gain, pre_shift, sub_gain, sub_shift, ffn_gain, ffn_shift], axis=1)).astype(f32).T
    mid = gather(jnp.stack([mid_gain, mid_shift], axis=1)).astype(f32).T
    wq = gather(qkv_weight)
    wo, fc1, fc2 = gather(out_weight), gather(fc1_weight), gather(fc2_weight)
    wown = lax.dynamic_index_in_dim(wq.reshape(D, 3, 2, W), tp, 2, keepdims=False).reshape(D, 3 * W)
    x = tokens.astype(f32)
    xh, xr = norm(x)
    a = (xh * small[0] + small[1]).astype(bf16)
    afull = lax.all_gather(a, "tp", axis=0, tiled=True)
    qkv = nn(afull, wown).astype(bf16)
    o_own, lse = attn_fwd(lengths, qkv, B=512)
    o = lax.all_to_all(o_own, "tp", 0, 1, tiled=True)
    vec = jnp.concatenate([small, jnp.zeros((2, D), f32)], axis=0)
    block_out, dy, do, delta, gwo, gfc1, gfc2, gvec, gmid = ffn(
        o, tokens, cotangent, wo, fc1, fc2, vec, jnp.concatenate([mid, jnp.zeros((6, 4 * D), f32)], axis=0))
    do_own = lax.all_to_all(do, "tp", 1, 0, tiled=True)
    dl_own = lax.all_to_all(delta, "tp", 0, 1, tiled=True)
    dqkv = attn_bwd(lengths, qkv, do_own, lse, dl_own, B=512)
    gq = tn(afull, dqkv)
    da = lax.psum_scatter(nt(dqkv, wown), "tp", scatter_dimension=0, tiled=True)
    grad_tokens = (dy.astype(f32) + ln_back(da, xh, xr, small[0])).astype(bf16)
    scatter = lambda v: lax.psum_scatter(v, both, scatter_dimension=0, tiled=True)
    gq = lax.psum_scatter(gq, "dp", scatter_dimension=0, tiled=True)
    n = gq.shape[0] // 2
    gq = lax.all_to_all(gq.reshape(2, n, 3, 1, W), "tp", 0, 3, tiled=True).reshape(n, 3 * D)
    small_grads = scatter(jnp.concatenate([jnp.stack([colsum(da * xh)[0], colsum(da)[0]]), gvec[2:6]], axis=0).T).T
    mid_grads = scatter(gmid[6:8].T).T
    gwo = scatter(gwo.astype(f32))
    gfc1 = scatter(gfc1.reshape(-1, D).astype(f32))
    gfc2 = scatter(gfc2.reshape(-1, D).astype(f32))
    return (block_out, grad_tokens, gq, gwo, small_grads[0], small_grads[1], small_grads[2], small_grads[3],
            small_grads[4], small_grads[5], gfc1, mid_grads[0], mid_grads[1], gfc2)


def local(*arrays):
    fits = lax.axis_size("dp") == 16 and lax.axis_size("tp") == 2
    return (local_fast if fits else local_any)(*arrays)


def solution(mesh):
    two, one = P(("dp", "tp"), None), P(("dp", "tp"))
    return jax.shard_map(
        local,
        mesh=mesh,
        in_specs=(two, two, P("dp", None), two, two, one, one, one, one, one, one, two, one, one, two),
        out_specs=(two, two, two, two, one, one, one, one, one, one, two, one, one, two),
        check_vma=False,
    )
```

profile of v0, /device:TPU:0, one launch (start us, length us, event | category | flops | bytes accessed | tf_op | source)
XLA Modules:
  0.0 279.7 jit_solution(1936049669563595310)
XLA Ops:
  0.6 0.8 stack.36
  1.4 0.7 fusion.6
  2.1 0.6 fusion.7.vpk
  2.7 88.3 %forward.1 = (bf16[1024,768]{1,0:T(8,128)(2,1)}, f32[3,2,2048]{2,1,0:T(2,128)}, f32[8,768]{1,0:T(8,128)}, f32[8,3072]{1,0:T(8,128)}, bf16[2048,768]{1,0:T(8,128)...) custom-call(s32[1,8]{1,0:T(1,128)} %len_ref.3, ...), custom_call_target="tpu_custom_call" | custom-call | tf_op jit(solution)/shard_map/forward/pallas_call | solution.py:621
  91.0 67.7 %ffn.1 = (f32[16,1024]{1,0:T(8,128)}, f32[8,768]{1,0:T(8,128)}, f32[8,3072]{1,0:T(8,128)}, bf16[6,512,768]{2,1,0:T(8,128)(2,1)}, bf16[6,512,768]{2,1,0:T(8,128)(...) custom-call(f32[8,768]{1,0:T(8,128)} %get-tuple-element.40.vec, ...), custom_call_target="tpu_custom_call" | custom-call | tf_op jit(solution)/shard_map/ffn/pallas_call | solution.py:354
  158.7 111.0 %backward.1 = (bf16[1024,768]{1,0:T(8,128)(2,1)}, f32[24,2304]{1,0:T(8,128)}, f32[24,768]{1,0:T(8,128)}, f32[96,768]{1,0:T(8,128)}, f32[96,768]{1,0:T(8,128)}, /*index=5*/f32[8,128]{1,0:T(8,128)}, f32[24,128]{1,0:T(8,128)}) custom-call(s32[1,8]{1,0:T(1,128)} %len_ref.3, bf16[1024,768]{1,0:T(8,128)(2,1)} %get-tuple-element.47.do, ...), custom_call_target="tpu_custom_call" | custom-call | tf_op jit(solution)/shard_map/backward/pallas_call | solution.py:922
  269.7 1.5 slice_reduce_fusion
  271.1 1.3 slice_bitcast_fusion
  272.4 1.3 slice_bitcast_fusion.2
  273.7 0.0 copy-start.2
  273.7 0.0 copy-start.3
  273.8 0.0 copy-start.1
  273.8 0.0 copy-start
  273.8 2.7 copy.40
  276.5 0.0 copy-done.2
  276.5 0.7 copy.41
  277.2 0.0 copy-done.3
  277.2 0.6 copy.42
  277.8 0.0 copy-done.1
  277.8 0.7 copy.43
  278.5 0.0 copy-done
  278.5 0.7 copy.44
Async XLA Ops:
  273.7 2.8 copy-start.2
  273.7 3.4 %copy-start.3 = (f32[24,768]{1,0:T(8,128)S(1)}, f32[24,768]{1,0:T(8,128)}, u32[]{:S(2)}) copy-start(f32[24,768]{1,0:T(8,128)} %get-tuple-element.91) | copy-start | bytes 221188
  273.8 4.1 %copy-start.1 = (f32[96,768]{1,0:T(8,128)S(1)}, f32[96,768]{1,0:T(8,128)}, u32[]{:S(2)}) copy-start(f32[96,768]{1,0:T(8,128)} %get-tuple-element.98) | copy-start | bytes 884740
  273.8 4.8 %copy-start = (f32[96,768]{1,0:T(8,128)S(1)}, f32[96,768]{1,0:T(8,128)}, u32[]{:S(2)}) copy-start(f32[96,768]{1,0:T(8,128)} %get-tuple-element.101) | copy-start | bytes 884740
where the time goes:
time: 278 us; the launch traced here: 280 us
  Pallas kernels  267 us (96%)
  local copies, waits for them, and re-layouts  10.3 us (4%)
    pallas_call x1, Pallas kernels, k45(): pl.pallas_call(functools.partial(k45_kernel, B=B, pairs=pairs), name='bac...  111 us
    pallas_call x1, Pallas kernels, k12(): pl.pallas_call(functools.partial(k12_kernel, B=B, pairs=pairs), name='for...  88.3 us
    pallas_call x1, Pallas kernels, ffn(): pl.pallas_call(functools.partial(ffn_kernel, T=T, NT=NT, NC=NC, SR=SR, UT...  67.7 us

commit v1 on v0

--- a/solution.py
+++ b/solution.py
@@ -712,7 +712,7 @@
     l_w = [pltpu.make_async_copy(wown_h.at[p], wown.at[:, p * 384:(p + 1) * 384], ls.at[7 + p]) for p in range(pairs)]
     for l in [l_q, l_2, l_o, l_1, l_x] + l_w + [l_t, l_y]: l.start()
     enter(w)
-    for c in (c_do, c_dl, c_ro, c_r2, c_r1): c.start()
+    for c in (c_do, c_dl): c.start()
     do_own[mine_rows, :] = do[:, mine_cols]
     dl_own[:, mine_rows] = delta[pl.ds(pl.multiple_of(tp * 8, 8), 8), :]
     doc_features(len_ref, 2 * rows, fq, fk)
@@ -731,6 +731,7 @@
     vacc[...] = jnp.zeros_like(vacc); uacc[...] = jnp.zeros_like(uacc)
     l_q.wait()
     c_do.wait_recv(); c_dl.wait_recv()
+    c_r2.start(); c_ro.start()
 
     half = lax.broadcasted_iota(jnp.int32, (1, 128), 1) < 64
     causal = lax.broadcasted_iota(jnp.int32, (B, B), 0) <= lax.broadcasted_iota(jnp.int32, (B, B), 1)
@@ -766,6 +767,7 @@
                 for k in range(4): s4[z, k] = sm[z, k, tp] + pm[z, k]
             fm.start()
             c_r2.wait_recv(); l_2.wait()
+            c_r1.start()
             for z in range(4):
                 for k in range(4): s2[z, k] = add(s2[z, k], r2[z, k])
             f2.start()
@@ -778,7 +780,6 @@
             c_r1.wait_recv(); l_1.wait()
             for z in range(4):
                 for k in range(4): s1[z, k] = add(s1[z, k], r1[z, k])
-            f1.start()
         @at(3)
         def _():
             fm.after_a()
@@ -787,29 +788,33 @@
             l_x.wait()
             for l in l_w: l.wait()
             grads(0)
-            f2.after_b(); fo_.after_b(); fqs[0].start()
+            f2.after_b(); fo_.after_b(); f1.start()
             small_o[...] = fm.result()
         @at(5)
         def _():
-            f2.after_a(); fo_.after_a()
+            fqs[0].start()
         @at(6)
         def _():
-            f1.after_b(); fqs[0].after_b()
+            fo_.after_a()
         @at(7)
         def _():
-            fqs[0].after_a()
+            f2.after_a(); fqs[0].after_b()
         @at(8)
         def _():
-            f1.after_a(); grads(1); fqs[1].start()
-            g2_o[...] = f2.result()
+            grads(1)
+            f1.after_b(); fqs[1].start()
+        @at(9)
+        def _():
+            f1.after_a(); fqs[0].after_a()
             fo[...] = fo_.result()
             c_xo.start()
-        @at(9)
+        @at(10)
         def _():
             fqs[1].after_b()
-        @at(10)
+        @at(11)
         def _():
             fqs[1].after_a()
+            g2_o[...] = f2.result()
         @pl.when(j == 0)
         def _():
             def prep(i, _):

time: 278 us -> 273 us (0.982)
  Pallas kernels: 267 us -> 262 us
    pallas_call x1, Pallas kernels: 111 us -> 106 us  [k45(): pl.pallas_call(functools.partial(k45_kernel, B=B, pairs=pairs), name='bac...]
where the time goes in v1:
time: 273 us; the launch traced here: 274 us
  Pallas kernels  262 us (96%)
  local copies, waits for them, and re-layouts  10.3 us (4%)
    pallas_call x1, Pallas kernels, k45(): pl.pallas_call(functools.partial(k45_kernel, B=B, pairs=pairs), name='bac...  106 us
    pallas_call x1, Pallas kernels, k12(): pl.pallas_call(functools.partial(k12_kernel, B=B, pairs=pairs), name='for...  88.3 us
    pallas_call x1, Pallas kernels, ffn(): pl.pallas_call(functools.partial(ffn_kernel, T=T, NT=NT, NC=NC, SR=SR, UT...  67.7 us
    unnamed x13, local copies, waits for them, and re-layouts  5.49 us

profile of v1, /device:TPU:0, one launch (start us, length us, event | category | flops | bytes accessed | tf_op | source)
XLA Modules:
  0.0 274.5 jit_solution(6673457223518678592)
XLA Ops:
  0.6 0.8 stack.36
  1.4 0.7 fusion.6
  2.1 0.6 fusion.7.vpk
  2.7 88.3 %forward.1 = (bf16[1024,768]{1,0:T(8,128)(2,1)}, f32[3,2,2048]{2,1,0:T(2,128)}, f32[8,768]{1,0:T(8,128)}, f32[8,3072]{1,0:T(8,128)}, bf16[2048,768]{1,0:T(8,128)...) custom-call(s32[1,8]{1,0:T(1,128)} %len_ref.3, ...), custom_call_target="tpu_custom_call" | custom-call | tf_op jit(solution)/shard_map/forward/pallas_call | solution.py:621
  91.0 67.7 %ffn.1 = (f32[16,1024]{1,0:T(8,128)}, f32[8,768]{1,0:T(8,128)}, f32[8,3072]{1,0:T(8,128)}, bf16[6,512,768]{2,1,0:T(8,128)(2,1)}, bf16[6,512,768]{2,1,0:T(8,128)(...) custom-call(f32[8,768]{1,0:T(8,128)} %get-tuple-element.40.vec, ...), custom_call_target="tpu_custom_call" | custom-call | tf_op jit(solution)/shard_map/ffn/pallas_call | solution.py:354
  158.7 106.1 %backward.1 = (bf16[1024,768]{1,0:T(8,128)(2,1)}, f32[24,2304]{1,0:T(8,128)}, f32[24,768]{1,0:T(8,128)}, f32[96,768]{1,0:T(8,128)}, f32[96,768]{1,0:T(8,128)}, /*index=5*/f32[8,128]{1,0:T(8,128)}, f32[24,128]{1,0:T(8,128)}) custom-call(s32[1,8]{1,0:T(1,128)} %len_ref.3, bf16[1024,768]{1,0:T(8,128)(2,1)} %get-tuple-element.47.do, ...), custom_call_target="tpu_custom_call" | custom-call | tf_op jit(solution)/shard_map/backward/pallas_call | solution.py:927
  264.8 1.5 slice_reduce_fusion
  266.2 1.3 slice_bitcast_fusion
  267.5 1.3 slice_bitcast_fusion.2
  268.8 0.0 copy-start.2
  268.8 0.0 copy-start.3
  268.8 0.0 copy-start.1
  268.9 0.0 copy-start
  268.9 2.7 copy.40
  271.6 0.0 copy-done.2
  271.6 0.7 copy.41
  272.3 0.0 copy-done.3
  272.3 0.6 copy.42
  272.9 0.0 copy-done.1
  272.9 0.7 copy.43
  273.6 0.0 copy-done
  273.6 0.7 copy.44
Async XLA Ops:
  268.8 2.8 %copy-start.2 = (f32[24,2304]{1,0:T(8,128)S(1)}, f32[24,2304]{1,0:T(8,128)}, u32[]{:S(2)}) copy-start(f32[24,2304]{1,0:T(8,128)} %get-tuple-element.90) | copy-start | bytes 663556
  268.8 3.4 %copy-start.3 = (f32[24,768]{1,0:T(8,128)S(1)}, f32[24,768]{1,0:T(8,128)}, u32[]{:S(2)}) copy-start(f32[24,768]{1,0:T(8,128)} %get-tuple-element.91) | copy-start | bytes 221188
  268.8 4.1 %copy-start.1 = (f32[96,768]{1,0:T(8,128)S(1)}, f32[96,768]{1,0:T(8,128)}, u32[]{:S(2)}) copy-start(f32[96,768]{1,0:T(8,128)} %get-tuple-element.98) | copy-start | bytes 884740
  268.9 4.8 %copy-start = (f32[96,768]{1,0:T(8,128)S(1)}, f32[96,768]{1,0:T(8,128)}, u32[]{:S(2)}) copy-start(f32[96,768]{1,0:T(8,128)} %get-tuple-element.101) | copy-start | bytes 884740

commit v2 on v1

--- a/solution.py
+++ b/solution.py
@@ -222,9 +222,13 @@
     ff, D = fc1.shape
     K = ff // NC
     NS = NT // UT
-    ins = [pltpu.make_async_copy(h, v, ws.at[k]) for k, (h, v) in enumerate(
-        ((o_h, o_ref), (wo_h, wo), (x_h, x_ref), (fc1_h, fc1), (g_h, g_ref), (fc2_h, fc2)))]
-    outs = [pltpu.make_async_copy(v, h, ws.at[6 + k]) for k, (h, v) in enumerate(
+    def parts(h, v, first, n):
+        m = v.shape[0] // n
+        return [pltpu.make_async_copy(h.at[k * m:(k + 1) * m, :], v.at[k * m:(k + 1) * m, :], ws.at[first + k]) for k in range(n)]
+    early = parts(o_h, o_ref, 0, 2) + parts(wo_h, wo, 2, 1) + parts(x_h, x_ref, 3, 2)
+    load1 = parts(fc1_h, fc1, 5, 6)
+    load2 = parts(g_h, g_ref, 11, 2) + parts(fc2_h, fc2, 13, 6)
+    outs = [pltpu.make_async_copy(v, h, ws.at[19 + k]) for k, (h, v) in enumerate(
         ((dy_h, dy_ref), (do_h, do_ref), (gwo_h, gwo)))]
     sg, sb, fg, fb = [vec[k:k + 1, :] for k in range(2, 6)]
     tiles = [slice(t * T, (t + 1) * T) for t in range(NT)]
@@ -236,9 +240,9 @@
         return r
     @pl.when(step == 0)
     def _():
-        for l in ins: l.start()
+        for l in early + load1 + load2: l.start()
         gvec[...] = jnp.zeros_like(gvec); gmid[...] = jnp.zeros_like(gmid)
-        ins[0].wait(); ins[1].wait(); ins[2].wait()
+        for l in early: l.wait()
         bs = []
         for sl in tiles:
             oh, _r = stats(o_ref[sl, :].astype(f32))
@@ -248,7 +252,7 @@
         for sl in tiles:
             yh, _r = stats(y_s[sl, :])
             c_s[sl, :] = (yh * fg + fb).astype(bf16)
-        ins[3].wait()
+        for l in load1: l.wait()
     base = jnp.minimum(step, NS - 1) * T
     rs = pl.ds(pl.multiple_of(base, T), T)
     sub_rows = lambda s: pl.ds(pl.multiple_of(base + s.start, SR), SR)
@@ -270,7 +274,7 @@
             if c + 1 < NC: h_s[(c + 1) % 2] = nt(c_s[rs, :], fc1[cols[c + 1], :])
     @pl.when(step == 0)
     def _():
-        ins[4].wait(); ins[5].wait()
+        for l in load2: l.wait()
     @pl.when(step < NS)
     def _():
         mu, R = moments()
@@ -361,7 +365,7 @@
                         M((D, D), bf16), M((ff, D), bf16), M((ff, D), bf16), M((rows, D), bf16), M((rows, D), bf16), M((D, D), bf16),
                         M((2, T, K), f32), M((T, ff), f32), M((T, ff), f32), M((T, ff), f32),
                         M((rows, ff), bf16), M((rows, ff), bf16), M((rows, D), bf16), M((rows, D), bf16), M((rows, D), f32), M((rows, D), f32),
-                        M((4, NC, T, 128), f32), pltpu.SemaphoreType.DMA((10,))],
+                        M((4, NC, T, 128), f32), pltpu.SemaphoreType.DMA((22,))],
         compiler_params=pltpu.CompilerParams(vmem_limit_bytes=63 << 20, dimension_semantics=("arbitrary",)))(
             vec, mid, sel, o, x, g, wo, fc1, fc2)
     return out, dy, do, delta, gwo, g1, g2, gvec, gmid
@@ -594,8 +598,8 @@
         return 0
     lax.fori_loop(0, pairs * nb, unit, 0)
     co[2].start()
+    o_out[:, cols] = o_loc[pl.ds(pl.multiple_of(tp * rows, rows), rows), :]
     g2.after_b()
-    o_out[:, cols] = o_loc[pl.ds(pl.multiple_of(tp * rows, rows), rows), :]
     got(co)
     go.finish(); g1.finish(); g2.finish()
     for c in send.all: c.wait_send()

time: 273 us -> 273 us (level)
  no operation moved by 1% of the time
where the time goes in v2:
time: 273 us; the launch traced here: 275 us
  Pallas kernels  262 us (96%)
  local copies, waits for them, and re-layouts  10.3 us (4%)
    pallas_call x1, Pallas kernels, k45(): pl.pallas_call(functools.partial(k45_kernel, B=B, pairs=pairs), name='bac...  106 us
    pallas_call x1, Pallas kernels, k12(): pl.pallas_call(functools.partial(k12_kernel, B=B, pairs=pairs), name='for...  88.3 us
    pallas_call x1, Pallas kernels, ffn(): pl.pallas_call(functools.partial(ffn_kernel, T=T, NT=NT, NC=NC, SR=SR, UT...  67.8 us
    unnamed x13, local copies, waits for them, and re-layouts  5.49 us

profile of v2, /device:TPU:0, one launch (start us, length us, event | category | flops | bytes accessed | tf_op | source)
XLA Modules:
  0.0 274.5 jit_solution(15893917550248506118)
XLA Ops:
  0.6 0.8 stack.36
  1.4 0.7 fusion.6
  2.1 0.6 fusion.7.vpk
  2.7 88.3 %forward.1 = (bf16[1024,768]{1,0:T(8,128)(2,1)}, f32[3,2,2048]{2,1,0:T(2,128)}, f32[8,768]{1,0:T(8,128)}, f32[8,3072]{1,0:T(8,128)}, bf16[2048,768]{1,0:T(8,128)...) custom-call(s32[1,8]{1,0:T(1,128)} %len_ref.3, ...), custom_call_target="tpu_custom_call" | custom-call | tf_op jit(solution)/shard_map/forward/pallas_call | solution.py:625
  91.0 67.8 %ffn.1 = (f32[16,1024]{1,0:T(8,128)}, f32[8,768]{1,0:T(8,128)}, f32[8,3072]{1,0:T(8,128)}, bf16[6,512,768]{2,1,0:T(8,128)(2,1)}, bf16[6,512,768]{2,1,0:T(8,128)(...) custom-call(f32[8,768]{1,0:T(8,128)} %get-tuple-element.40.vec, ...), custom_call_target="tpu_custom_call" | custom-call | tf_op jit(solution)/shard_map/ffn/pallas_call | solution.py:358
  158.8 105.8 %backward.1 = (bf16[1024,768]{1,0:T(8,128)(2,1)}, f32[24,2304]{1,0:T(8,128)}, f32[24,768]{1,0:T(8,128)}, f32[96,768]{1,0:T(8,128)}, f32[96,768]{1,0:T(8,128)}, /*index=5*/f32[8,128]{1,0:T(8,128)}, f32[24,128]{1,0:T(8,128)}) custom-call(s32[1,8]{1,0:T(1,128)} %len_ref.3, bf16[1024,768]{1,0:T(8,128)(2,1)} %get-tuple-element.47.do, ...), custom_call_target="tpu_custom_call" | custom-call | tf_op jit(solution)/shard_map/backward/pallas_call | solution.py:931
  264.7 1.5 slice_reduce_fusion
  266.2 1.3 slice_bitcast_fusion
  267.4 1.3 slice_bitcast_fusion.2
  268.8 0.0 copy-start.2
  268.8 0.0 copy-start.3
  268.8 0.0 copy-start.1
  268.8 0.0 copy-start
  268.8 2.7 copy.40
  271.5 0.0 copy-done.2
  271.5 0.7 copy.41
  272.2 0.0 copy-done.3
  272.2 0.6 copy.42
  272.9 0.0 copy-done.1
  272.9 0.7 copy.43
  273.6 0.0 copy-done
  273.6 0.7 copy.44
Async XLA Ops:
  268.8 2.8 %copy-start.2 = (f32[24,2304]{1,0:T(8,128)S(1)}, f32[24,2304]{1,0:T(8,128)}, u32[]{:S(2)}) copy-start(f32[24,2304]{1,0:T(8,128)} %get-tuple-element.90) | copy-start | bytes 663556
  268.8 3.4 %copy-start.3 = (f32[24,768]{1,0:T(8,128)S(1)}, f32[24,768]{1,0:T(8,128)}, u32[]{:S(2)}) copy-start(f32[24,768]{1,0:T(8,128)} %get-tuple-element.91) | copy-start | bytes 221188
  268.8 4.1 %copy-start.1 = (f32[96,768]{1,0:T(8,128)S(1)}, f32[96,768]{1,0:T(8,128)}, u32[]{:S(2)}) copy-start(f32[96,768]{1,0:T(8,128)} %get-tuple-element.98) | copy-start | bytes 884740
  268.8 4.8 %copy-start = (f32[96,768]{1,0:T(8,128)S(1)}, f32[96,768]{1,0:T(8,128)}, u32[]{:S(2)}) copy-start(f32[96,768]{1,0:T(8,128)} %get-tuple-element.101) | copy-start | bytes 884740
